TPU v7x, 512 devices: a whole 4x4x16 slice. The times are simulated.
512 devices in a mesh: ctx: 32 (over y_hi, z), tp: 16 (over y_lo, x, core).
Axes of the slice: x: 4, y: 4 (y_hi: 2, y_lo: 2; y = y_hi * 2 + y_lo), z: 16, core: 2. Of those that a mesh axis runs over, the one named last changes fastest.
Arguments:
- query_rows: bfloat16 [4096, 1024], P('ctx', 'tp'), may hold values from -12 to 12
- key_rows: bfloat16 [4096, 1024], P('ctx', 'tp'), may hold values from -6 to 6
- value_rows: bfloat16 [4096, 1024], P('ctx', 'tp'), may hold values from -6 to 6
- valid_frames: int32 [1], replicated, may hold values from 3072 to 4096
- depth_kernel: float32 [32, 1024], P(None, 'tp'), may hold values from -1 to 1
- mix_weight: bfloat16 [1024, 1536], P('tp'), may hold values from -0.1875 to 0.1875
- out_grad: bfloat16 [4096, 1536], P(('ctx', 'tp')), may hold values from -6 to 6
Outputs:
- block_out: bfloat16 [4096, 1536], P(('ctx', 'tp'))
- query_grad: bfloat16 [4096, 1024], P('ctx', 'tp')
- key_grad: bfloat16 [4096, 1024], P('ctx', 'tp')
- value_grad: bfloat16 [4096, 1024], P('ctx', 'tp')
- mix_grad: float32 [1024, 1536], P('tp')
- kernel_grad: float32 [32, 1024], P(None, 'tp')
Inputs may be any that keep to these rules, and one draw needn't show every extreme that they name: Frames from valid_frames on are padding.
All inputs are finite; a program needn't handle non-finite values.
Results may differ from a plain program's by a relative error of at most 0.039.
Values may be sent and summed in bfloat16 or wider, within the bound.
No kernel may reach another device: no remote copies, remote signals or barrier semaphores. Data moves between devices by JAX's collectives and lax.ppermute only.
A program may use at most 64 MiB of HBM per device.

v0:
```python
import jax
import jax.numpy as jnp
from jax import lax
from jax.sharding import PartitionSpec as P

KSIZE = 32


def with_halo(block, sides, width):
    for axis, dim in sides:
        count = lax.axis_size(axis)
        forward = [(i, i + 1) for i in range(count - 1)]
        backward = [(target, source) for source, target in forward]
        low = lax.ppermute(
            lax.slice_in_dim(block, block.shape[dim] - width, None, axis=dim), axis, forward
        )
        high = lax.ppermute(lax.slice_in_dim(block, 0, width, axis=dim), axis, backward)
        block = jnp.concatenate([low, block, high], axis=dim)
    return block


def body(query_rows, key_rows, value_rows, valid_frames, depth_kernel, mix_weight, out_grad):
    frames_dev = query_rows.shape[0]
    head_width = query_rows.shape[1]
    score_scale = head_width ** (-0.5)
    total_frames = frames_dev * lax.axis_size("ctx")
    grad_norm = total_frames ** (-0.5)
    valid_count = valid_frames[0]
    own_ids = lax.axis_index("ctx") * frames_dev + jnp.arange(frames_dev, dtype=jnp.int32)
    own_live = own_ids < valid_count
    key_value = jnp.concatenate([key_rows, value_rows], axis=1)
    contract_last = (((1,), (1,)), ((), ()))
    key_piece = lax.all_gather(key_rows, "ctx", axis=0, tiled=True)
    run_max = jnp.full((frames_dev,), -1e30, jnp.float32)
    key_part = key_piece
    key_live = jnp.arange(key_piece.shape[0], dtype=jnp.int32) < valid_count
    scores = score_scale * lax.dot_general(
        query_rows, key_part, contract_last, preferred_element_type=jnp.float32
    )
    capped = jnp.where(key_live[None, :], scores, -1e30)
    new_max = jnp.maximum(run_max, jnp.max(capped, axis=1))
    weights = jnp.where(key_live[None, :], jnp.exp(capped - new_max[:, None]), 0.0)
    run_total = jnp.sum(weights, axis=1)
    run_max, run_total = (new_max, run_total)
    log_total = run_max + jnp.log(run_total)
    key_piece = lax.all_gather(key_value, "ctx", axis=0, tiled=True)
    key_part = key_piece[:, :head_width]
    value_part = key_piece[:, head_width:]
    key_live = jnp.arange(key_piece.shape[0], dtype=jnp.int32) < valid_count
    scores = score_scale * lax.dot_general(
        query_rows, key_part, contract_last, preferred_element_type=jnp.float32
    )
    capped = jnp.where(key_live[None, :], scores, -1e30)
    probs = jnp.where(key_live[None, :], jnp.exp(capped - log_total[:, None]), 0.0).astype(
        jnp.bfloat16
    )
    run_out = jnp.dot(probs, value_part, preferred_element_type=jnp.float32)
    attn = run_out.astype(jnp.bfloat16)
    masked = jnp.where(own_live[:, None], attn, jnp.zeros_like(attn))
    rim_width = KSIZE // 2
    padded_attn = with_halo(masked, (("ctx", 0),), rim_width)
    depth_out = jnp.zeros((frames_dev, head_width), jnp.float32)
    for offset in range(KSIZE):
        depth_out = depth_out + depth_kernel[offset][None, :] * padded_attn[
            offset : offset + frames_dev
        ].astype(jnp.float32)
    swished = (depth_out * jax.nn.sigmoid(depth_out)).astype(jnp.bfloat16)
    channel_rows = lax.all_to_all(swished, "tp", split_axis=0, concat_axis=1, tiled=True)
    full_weight = lax.all_gather(mix_weight, "tp", axis=0, tiled=True)
    block_out = jnp.dot(channel_rows, full_weight, preferred_element_type=jnp.float32).astype(
        jnp.bfloat16
    )
    grad_block = lax.all_gather(out_grad, "tp", axis=0, tiled=True)
    mix_back = lax.dot_general(
        grad_block, mix_weight, contract_last, preferred_element_type=jnp.float32
    )
    gate_sig = jax.nn.sigmoid(depth_out)
    depth_grad = (mix_back * gate_sig * (1.0 + depth_out * (1.0 - gate_sig))).astype(jnp.bfloat16)
    mix_part = lax.dot_general(
        swished, grad_block, (((0,), (0,)), ((), ())), preferred_element_type=jnp.float32
    )
    depth_grad_wide = depth_grad.astype(jnp.float32)
    kernel_rows = []
    for offset in range(KSIZE):
        kernel_rows.append(
            jnp.sum(
                padded_attn[offset : offset + frames_dev].astype(jnp.float32) * depth_grad_wide,
                axis=0,
            )
        )
    kernel_part = jnp.stack(kernel_rows, axis=0)
    mix_total, kernel_total = (
        lax.psum(mix_part.astype(jnp.bfloat16), "ctx").astype(jnp.float32),
        lax.psum(kernel_part.astype(jnp.bfloat16), "ctx").astype(jnp.float32),
    )
    mix_grad = grad_norm * mix_total
    kernel_grad = grad_norm * kernel_total
    padded_grad = with_halo(depth_grad, (("ctx", 0),), rim_width)
    back_sum = jnp.zeros((frames_dev, head_width), jnp.float32)
    for offset in range(KSIZE):
        first_row = 2 * rim_width - offset
        back_sum = back_sum + depth_kernel[offset][None, :] * padded_grad[
            first_row : first_row + frames_dev
        ].astype(jnp.float32)
    attn_grad = jnp.where(own_live[:, None], back_sum, jnp.zeros_like(back_sum)).astype(
        jnp.bfloat16
    )
    delta = jnp.sum(attn_grad.astype(jnp.float32) * attn.astype(jnp.float32), axis=1)
    key_piece = lax.all_gather(key_value, "ctx", axis=0, tiled=True)
    key_part = key_piece[:, :head_width]
    value_part = key_piece[:, head_width:]
    key_live = jnp.arange(key_piece.shape[0], dtype=jnp.int32) < valid_count
    scores = score_scale * lax.dot_general(
        query_rows, key_part, contract_last, preferred_element_type=jnp.float32
    )
    capped = jnp.where(key_live[None, :], scores, -1e30)
    weights = jnp.where(key_live[None, :], jnp.exp(capped - log_total[:, None]), 0.0)
    dprobs = lax.dot_general(
        attn_grad, value_part, contract_last, preferred_element_type=jnp.float32
    )
    dscores = (weights * (dprobs - delta[:, None])).astype(jnp.bfloat16)
    query_total = score_scale * jnp.dot(dscores, key_part, preferred_element_type=jnp.float32)
    query_grad = query_total.astype(jnp.bfloat16)
    query_and_grad = jnp.concatenate([query_rows, attn_grad], axis=1)
    row_stats = jnp.stack([log_total, delta], axis=1)
    all_stats = lax.all_gather(row_stats, "ctx", axis=0, tiled=True)
    rows_piece = lax.all_gather(query_and_grad, "ctx", axis=0, tiled=True)
    query_piece = rows_piece[:, :head_width]
    grad_piece = rows_piece[:, head_width:]
    total_piece = all_stats[:, 0]
    delta_piece = all_stats[:, 1]
    scores = score_scale * lax.dot_general(
        key_rows, query_piece, contract_last, preferred_element_type=jnp.float32
    )
    capped = jnp.where(own_live[:, None], scores, -1e30)
    weights = jnp.where(own_live[:, None], jnp.exp(capped - total_piece[None, :]), 0.0)
    dprobs = lax.dot_general(
        value_rows, grad_piece, contract_last, preferred_element_type=jnp.float32
    )
    dscores = (weights * (dprobs - delta_piece[None, :])).astype(jnp.bfloat16)
    key_total = score_scale * jnp.dot(dscores, query_piece, preferred_element_type=jnp.float32)
    value_total = jnp.dot(
        weights.astype(jnp.bfloat16), grad_piece, preferred_element_type=jnp.float32
    )
    key_total, value_total = (key_total, value_total)
    return (
        block_out,
        query_grad,
        key_total.astype(jnp.bfloat16),
        value_total.astype(jnp.bfloat16),
        mix_grad,
        kernel_grad,
    )


def solution(mesh):
    placed = (
        P("ctx", "tp"),
        P("ctx", "tp"),
        P("ctx", "tp"),
        P(),
        P(None, "tp"),
        P("tp", None),
        P(("ctx", "tp"), None),
    )
    return jax.shard_map(
        body,
        mesh=mesh,
        in_specs=placed,
        out_specs=(
            P(("ctx", "tp"), None),
            P("ctx", "tp"),
            P("ctx", "tp"),
            P("ctx", "tp"),
            P("tp", None),
            P(None, "tp"),
        ),
        check_vma=False,
    )
```

profile of v0, /device:TPU:1, one launch (start us, length us, event | category | flops | bytes accessed | tf_op | source)
XLA Modules:
  0.0 650.3 jit_solution(8706354773599395544)
XLA Ops:
  7.2 0.0 all-gather.4.cloned.1.call-start
  7.2 1.4 pad_maximum_fusion
  8.6 0.0 all-gather.4.cloned.1.call-update
  8.6 0.0 all-reduce.2.cloned.1.call-start
  9.3 72.7 %all_gather.20 = bf16[4096,64]{0,1:T(8,128)(2,1)S(1)} all-gather(bf16[128,64]{0,1:T(8,128)(2,1)} %param.8), channel_id=1, replica_groups=mesh['ctx'=32,'tp'=16] {'ctx'}, dimensions={0}, use_global_device_ids=true | all-gather | bytes 540672 | tf_op jit(solution)/shard_map/all_gather | solution.py:33
  82.1 1.3 fusion.177
  83.4 0.5 select_reduce_fusion
  84.0 0.0 copy-done.7
  84.0 58.7 %all-gather.4.cloned.1.call-done = bf16[4096,128]{0,1:T(8,128)(2,1)} async-done(((bf16[128,128]{0,1:T(8,128)(2,1)}), bf16[4096,128]{0,1:T(8,128)(2,1)}) %all-gather.4.cloned.1.call-update) | async-done | bytes 1048592 | tf_op jit(solution)/shard_map/all_gather | solution.py:46
  142.7 0.0 copy-done.3
  142.7 3.0 fusion.8
  145.7 0.0 copy-done.1
  145.7 0.0 copy-start.6
  145.7 0.0 copy-start.2
  145.7 0.3 broadcast_select_fusion
  146.0 0.1 fusion.176
  146.1 1.3 collective-permute-start.1
  147.4 4.0 collective-permute-start
  151.4 0.0 copy-done.6
  151.4 30.7 %all_gather.22 = bf16[128,1536]{1,0:T(8,128)(2,1)S(1)} all-gather(bf16[8,1536]{1,0:T(8,128)(2,1)S(1)} %copy-done.6), channel_id=1, replica_groups=mesh['ctx'=32,'tp'=16] {'tp'}, dimensions={0}, use_global_device_ids=true | all-gather | bytes 417792 | tf_op jit(solution)/shard_map/all_gather | solution.py:73
  182.1 0.0 collective-permute-done.1
  182.1 0.0 collective-permute-done
  182.1 0.6 multiply_convert_fusion
  182.7 0.0 copy-done.2
  182.7 0.5 fusion.97
  183.2 0.1 fusion.175
  183.3 2.9 collective-permute-start.3
  186.2 1.3 collective-permute-start.2
  187.5 0.9 convolution_convert_fusion
  188.4 0.0 all-reduce.2.cloned.1.call-update
  188.4 0.0 all-gather.8.cloned.1.call-start
  188.4 0.0 collective-permute-done.3
  188.5 2.2 collective-permute-done.2
  190.7 0.6 multiply_reduce_fusion
  191.3 0.6 pad_maximum_fusion.1
  191.9 0.0 all-gather.8.cloned.1.call-update
  191.9 0.0 all-gather.6.cloned.1.call-start
  192.0 0.5 all-gather.6.cloned.1.call-update
  192.5 0.1 copy.13
  192.6 0.7 reshape.50
  193.3 4.9 all-to-all-start
  198.2 0.3 fusion.113
  198.6 0.4 fusion.98
  198.9 0.4 fusion.114
  199.3 0.1 stack.170
  199.5 62.3 %psum.15 = bf16[32,64]{1,0:T(8,128)(2,1)S(1)} all-reduce(bf16[32,64]{1,0:T(8,128)(2,1)S(1)} %stack.170), channel_id=1, replica_groups=mesh['ctx'=32,'tp'=16] {'ctx'}, use_global_device_ids=true, to_apply=%region_36.37 | all-reduce | flops 2048 | bytes 8192 | tf_op jit(solution)/shard_map/psum | solution.py:94
  261.8 0.6 convert_multiply_fusion.66
  262.4 58.0 %all_gather.24 = f32[4096,2]{0,1:T(2,128)S(1)} all-gather(f32[128,2]{0,1:T(2,128)S(1)} %pad_maximum_fusion.6), channel_id=1, replica_groups=mesh['ctx'=32,'tp'=16] {'ctx'}, dimensions={0}, use_global_device_ids=true | all-gather | bytes 33792 | tf_op jit(solution)/shard_map/all_gather | solution.py:126
  320.4 1.4 fusion.21
  321.9 0.0 all-to-all-done
  321.9 0.1 reshape.51
  322.0 0.1 all_to_all.17
  322.1 127.2 %all-reduce.2.cloned.1.call-done = bf16[64,1536]{1,0:T(8,128)(2,1)} async-done(((bf16[64,1536]{1,0:T(8,128)(2,1)}), bf16[64,1536]{1,0:T(8,128)(2,1)}) %all-reduce.2.cloned.1.call-update) | async-done | bytes 196624 | tf_op jit(solution)/shard_map/psum | solution.py:93
  449.3 1.7 convert_multiply_fusion
  451.0 139.8 %all-gather.8.cloned.1.call-done = bf16[4096,128]{0,1:T(8,128)(2,1)} async-done(((bf16[128,128]{0,1:T(8,128)(2,1)}), bf16[4096,128]{0,1:T(8,128)(2,1)}) %all-gather.8.cloned.1.call-update) | async-done | bytes 1048592 | tf_op jit(solution)/shard_map/all_gather | solution.py:127
  590.8 0.0 copy-done.5
  590.8 2.1 fusion.11
  592.9 0.0 copy-done
  592.9 0.0 copy-start.4
  592.9 0.9 convolution_convert_fusion.2
  593.8 0.0 copy-done.4
  593.8 1.7 fusion.20
  595.5 45.2 %all-gather.6.cloned.1.call-done = bf16[1024,1536]{1,0:T(8,128)(2,1)} async-done(((bf16[64,1536]{1,0:T(8,128)(2,1)}), bf16[1024,1536]{1,0:T(8,128)(2,1)}) %all-gather.6.cloned.1.call-update) | async-done | bytes 3145744 | tf_op jit(solution)/shard_map/all_gather | solution.py:69
  640.7 3.0 convolution_convert_fusion.1
  (14 shorter events, 0.1 us)
Async XLA Ops:
  7.2 135.6 %all-gather.4.cloned.1.call-start = ((), (), s32[]{:S(2)}) async-start(), calls=%async_computation.1 | async-start | bytes 1081344 | tf_op jit(solution)/shard_map/all_gather | solution.py:46
  8.6 440.7 %all-reduce.2.cloned.1.call-start = ((), (), s32[]{:S(2)}) async-start(), calls=%async_computation.4 | async-start | bytes 393216 | tf_op jit(solution)/shard_map/psum | solution.py:93
  82.1 1.9 copy-start.7
  82.1 60.7 %copy-start.3 = (bf16[128,64]{0,1:T(8,128)(2,1)S(1)}, bf16[128,64]{0,1:T(8,128)(2,1)}, u32[]{:S(2)}) copy-start(bf16[128,64]{0,1:T(8,128)(2,1)} %param.7) | copy-start | bytes 49156
  142.7 3.0 copy-start.1
  145.7 5.7 copy-start.6
  145.7 37.0 %copy-start.2 = (bf16[64,1536]{1,0:T(8,128)(2,1)S(1)}, bf16[64,1536]{1,0:T(8,128)(2,1)}, u32[]{:S(2)}) copy-start(bf16[64,1536]{1,0:T(8,128)(2,1)} %param.12) | copy-start | bytes 589828
  146.1 36.0 %collective-permute-start.1 = (bf16[16,64]{0,1:T(8,128)(2,1)S(1)}, bf16[16,64]{0,1:T(8,128)(2,1)S(1)}, u32[]{:S(2)}, u32[]{:S(2)}) collective-permute-start(bf16[16,64]{0,1:T(8,128)(2,1)S(1)} %get-tuple-element.79), channel_id=1, source_target_pairs={{16,0},{32,16},{48,32},{64,48},{80,64},{96,80},{112,96},{128,112},... | collective-permute-start | bytes 6152 | tf_op jit(solution)/shard_map/ppermute | solution.py:17
  147.4 34.7 %collective-permute-start = (bf16[16,64]{0,1:T(8,128)(2,1)S(1)}, bf16[16,64]{0,1:T(8,128)(2,1)S(1)}, u32[]{:S(2)}, u32[]{:S(2)}) collective-permute-start(bf16[16,64]{0,1:T(8,128)(2,1)S(1)} %get-tuple-element.78), channel_id=1, source_target_pairs={{0,16},{16,32},{32,48},{48,64},{64,80},{80,96},{96,112},{112,128},... | collective-permute-start | bytes 6152 | tf_op jit(solution)/shard_map/ppermute | solution.py:14
  183.3 5.2 collective-permute-start.3
  186.2 4.5 collective-permute-start.2
  188.4 402.4 %all-gather.8.cloned.1.call-start = ((), (), s32[]{:S(2)}) async-start(), calls=%async_computation.3 | async-start | bytes 1081344 | tf_op jit(solution)/shard_map/all_gather | solution.py:127
  191.9 448.8 %all-gather.6.cloned.1.call-start = ((), (), s32[]{:S(2)}) async-start(), calls=%async_computation.2 | async-start | bytes 3342336 | tf_op jit(solution)/shard_map/all_gather | solution.py:69
  193.3 128.5 %all-to-all-start = ((bf16[16,2,256]{2,1,0:T(2,128)(2,1)}), bf16[16,2,256]{2,1,0:T(2,128)(2,1)S(1)}, u32[]{:S(2)}, u32[]{:S(2)}) async-start(bf16[16,2,256]{2,1,0:T(2,128)(2,1)} %reshape.50), calls=%async_computation | async-start | bytes 32768 | tf_op jit(solution)/shard_map/all_to_all | solution.py:68
  199.3 391.5 %copy-start.5 = (bf16[128,64]{0,1:T(8,128)(2,1)S(1)}, bf16[128,64]{0,1:T(8,128)(2,1)}, u32[]{:S(2)}) copy-start(bf16[128,64]{0,1:T(8,128)(2,1)} %param.8) | copy-start | bytes 49156
  590.8 2.1 copy-start
  592.9 0.9 copy-start.4
Sparse Core Ops, SparseCore 0:
  11.5 131.2 all-gather.3
  188.5 260.7 all-reduce.1
  452.6 138.1 all-gather.7
  593.0 47.6 all-gather.5
where the time goes:
time: 651 us; the launch traced here: 650 us
  waiting for transfers between devices  374 us (57%)
  blocking collectives  224 us (34%)
  matrix products  15 us (2%)
  between operations  14.6 us (2%)
  starting transfers between devices  14.5 us (2%)
  other arithmetic  7.18 us (1%)
    all_gather x1, waiting for transfers between devices, body(): rows_piece = lax.all_gather(query_and_grad, 'ctx', axis=0, tiled=True)  140 us
    psum x1, waiting for transfers between devices, body(): lax.psum(mix_part.astype(jnp.bfloat16), 'ctx').astype(jnp.float32)  127 us
    all_gather x1, blocking collectives, body(): key_piece = lax.all_gather(key_rows, 'ctx', axis=0, tiled=True)  72.7 us
    psum x1, blocking collectives, body(): lax.psum(kernel_part.astype(jnp.bfloat16), 'ctx').astype(jnp.float32)  62.3 us
    all_gather x1, waiting for transfers between devices, body(): key_piece = lax.all_gather(key_value, 'ctx', axis=0, tiled=True)  58.7 us
    all_gather x1, blocking collectives, body(): all_stats = lax.all_gather(row_stats, 'ctx', axis=0, tiled=True)  58 us
    all_gather x1, waiting for transfers between devices, body(): full_weight = lax.all_gather(mix_weight, 'tp', axis=0, tiled=True)  45.2 us
    all_gather x1, blocking collectives, body(): grad_block = lax.all_gather(out_grad, 'tp', axis=0, tiled=True)  30.7 us
  transfers between devices with their start and end apart: 9, of which 5 were waited for; matrix products, arithmetic and copies ran while one was open for 2% of the time, Pallas kernels for 0%

commit v1 on v0

--- a/solution.py
+++ b/solution.py
@@ -124,7 +124,9 @@
     query_and_grad = jnp.concatenate([query_rows, attn_grad], axis=1)
     row_stats = jnp.stack([log_total, delta], axis=1)
     all_stats = lax.all_gather(row_stats, "ctx", axis=0, tiled=True)
-    rows_piece = lax.all_gather(query_and_grad, "ctx", axis=0, tiled=True)
+    rows_piece = jnp.concatenate(
+        lax.all_to_all(jnp.stack([query_and_grad] * lax.axis_size("ctx")), "ctx", 0, 0), axis=0
+    )
     query_piece = rows_piece[:, :head_width]
     grad_piece = rows_piece[:, head_width:]
     total_piece = all_stats[:, 0]

time: 651 us -> 489 us (0.75)
  the two profiles are of different devices: /device:TPU:1 before, /device:TPU:2 now
where the time goes in v1:
time: 489 us
  blocking collectives  289 us (59%)
  waiting for transfers between devices  130 us (27%)
  starting transfers between devices  27.7 us (6%)
  between operations  16.4 us (3%)
  matrix products  16 us (3%)
  other arithmetic  6.6 us (1%)
    psum x1, blocking collectives, body(): lax.psum(kernel_part.astype(jnp.bfloat16), 'ctx').astype(jnp.float32)  115 us
    all_gather x1, blocking collectives, body(): key_piece = lax.all_gather(key_rows, 'ctx', axis=0, tiled=True)  85.7 us
    psum x1, waiting for transfers between devices, body(): lax.psum(mix_part.astype(jnp.bfloat16), 'ctx').astype(jnp.float32)  71 us
    all_gather x1, blocking collectives, body(): all_stats = lax.all_gather(row_stats, 'ctx', axis=0, tiled=True)  70.5 us
    all_gather x1, waiting for transfers between devices, body(): key_piece = lax.all_gather(key_value, 'ctx', axis=0, tiled=True)  54.9 us
    all_gather x1, blocking collectives, body(): grad_block = lax.all_gather(out_grad, 'tp', axis=0, tiled=True)  17.5 us
    all_to_all x1, starting transfers between devices, body(): lax.all_to_all(jnp.stack([query_and_grad] * lax.axis_size('ctx')), 'ctx',...  11.2 us
  transfers between devices with their start and end apart: 9, of which 3 were waited for; matrix products, arithmetic and copies ran while one was open for 3% of the time, Pallas kernels for 0%

profile of v1, /device:TPU:2, one launch (start us, length us, event | category | flops | bytes accessed | tf_op | source)
XLA Modules:
  0.0 488.8 jit_solution(15760486915014571643)
XLA Ops:
  8.0 0.0 all-gather.3.cloned.1.call-start
  8.0 1.4 pad_maximum_fusion
  9.4 0.0 all-gather.3.cloned.1.call-update
  9.4 0.0 all-reduce.2.cloned.1.call-start
  10.1 85.7 %all_gather.17 = bf16[4096,64]{0,1:T(8,128)(2,1)S(1)} all-gather(bf16[128,64]{0,1:T(8,128)(2,1)} %param.8), channel_id=1, replica_groups=mesh['ctx'=32,'tp'=16] {'ctx'}, dimensions={0}, use_global_device_ids=true | all-gather | bytes 540672 | tf_op jit(solution)/shard_map/all_gather | solution.py:33
  95.8 0.0 copy-start.2
  95.8 1.3 fusion.177
  97.2 0.5 select_reduce_fusion
  97.7 0.0 copy-done.6
  97.8 54.9 %all-gather.3.cloned.1.call-done = bf16[4096,128]{0,1:T(8,128)(2,1)} async-done(((bf16[128,128]{0,1:T(8,128)(2,1)}), bf16[4096,128]{0,1:T(8,128)(2,1)}) %all-gather.3.cloned.1.call-update) | async-done | bytes 1048592 | tf_op jit(solution)/shard_map/all_gather | solution.py:46
  152.7 0.0 copy-done.2
  152.7 0.0 copy-start
  152.7 3.0 fusion.11
  155.6 0.0 copy-done
  155.6 0.0 copy-start.5
  155.6 0.0 copy-start.1
  155.7 0.3 broadcast_select_fusion
  156.0 0.1 fusion.176
  156.0 1.3 collective-permute-start.1
  157.3 4.5 collective-permute-start
  161.9 0.0 copy-done.5
  161.9 17.5 %all_gather.19 = bf16[128,1536]{1,0:T(8,128)(2,1)S(1)} all-gather(bf16[8,1536]{1,0:T(8,128)(2,1)S(1)} %copy-done.5), channel_id=1, replica_groups=mesh['ctx'=32,'tp'=16] {'tp'}, dimensions={0}, use_global_device_ids=true | all-gather | bytes 417792 | tf_op jit(solution)/shard_map/all_gather | solution.py:73
  179.4 0.0 collective-permute-done.1
  179.4 0.0 collective-permute-done
  179.4 0.6 multiply_convert_fusion
  180.1 0.9 convolution_convert_fusion
  180.9 0.0 all-reduce.2.cloned.1.call-update
  181.0 0.0 all-gather.5.cloned.1.call-start
  181.0 0.5 all-gather.5.cloned.1.call-update
  181.5 0.0 copy-done.1
  181.6 0.5 fusion.97
  182.0 0.1 fusion.175
  182.1 3.2 collective-permute-start.3
  185.3 1.3 collective-permute-start.2
  186.6 0.1 copy.14
  186.7 0.7 reshape.56
  187.4 6.0 %all-to-all-start = ((bf16[16,2,256]{2,1,0:T(2,128)(2,1)}), bf16[16,2,256]{2,1,0:T(2,128)(2,1)S(1)}, u32[]{:S(2)}, u32[]{:S(2)}) async-start(bf16[16,2,256]{2,1,0:T(2,128)(2,1)} %reshape.56), calls=%async_computation | async-start | bytes 32768 | tf_op jit(solution)/shard_map/all_to_all | solution.py:68
  193.4 0.0 collective-permute-done.3
  193.4 0.0 collective-permute-done.2
  193.4 0.6 multiply_reduce_fusion
  194.1 0.1 copy.16
  194.2 4.0 all-to-all-done
  198.2 1.2 stack.172
  199.4 11.2 %all-to-all-start.1 = ((bf16[32,128,128]{2,1,0:T(8,128)(2,1)}), bf16[32,128,128]{2,1,0:T(8,128)(2,1)S(1)}, u32[]{:S(2)}, u32[]{:S(2)}) async-start(bf16[32,128,128]{2,1,0:T(8,128)(2,1)} %stack.172), calls=%async_computation.1 | async-start | bytes 2097152 | tf_op jit(solution)/shard_map/all_to_all | solution.py:128
  210.7 0.3 fusion.113
  211.0 0.4 fusion.98
  211.4 0.4 fusion.114
  211.8 0.1 stack.206
  211.9 115.4 %psum.15 = bf16[32,64]{1,0:T(8,128)(2,1)S(1)} all-reduce(bf16[32,64]{1,0:T(8,128)(2,1)S(1)} %stack.206), channel_id=1, replica_groups=mesh['ctx'=32,'tp'=16] {'ctx'}, use_global_device_ids=true, to_apply=%region_36.37 | all-reduce | flops 2048 | bytes 8192 | tf_op jit(solution)/shard_map/psum | solution.py:94
  327.3 0.6 convert_multiply_fusion.66
  327.9 70.5 %all_gather.20 = f32[4096,2]{0,1:T(2,128)S(1)} all-gather(f32[128,2]{0,1:T(2,128)S(1)} %pad_maximum_fusion.6), channel_id=1, replica_groups=mesh['ctx'=32,'tp'=16] {'ctx'}, dimensions={0}, use_global_device_ids=true | all-gather | bytes 33792 | tf_op jit(solution)/shard_map/all_gather | solution.py:126
  398.4 2.6 fusion.20
  401.1 0.1 reshape.57
  401.2 0.1 all_to_all.20
  401.3 71.0 %all-reduce.2.cloned.1.call-done = bf16[64,1536]{1,0:T(8,128)(2,1)} async-done(((bf16[64,1536]{1,0:T(8,128)(2,1)}), bf16[64,1536]{1,0:T(8,128)(2,1)}) %all-reduce.2.cloned.1.call-update) | async-done | bytes 196624 | tf_op jit(solution)/shard_map/psum | solution.py:93
  472.2 1.7 convert_multiply_fusion
  474.0 3.0 convolution_convert_fusion.1
  477.0 0.0 all-to-all-done.1
  477.0 0.0 copy-done.4
  477.0 0.8 fusion.4
  477.8 0.0 copy-start.3
  477.8 1.6 convolution_convert_fusion.3
  479.4 0.0 copy-done.3
  479.4 1.9 fusion.21
  (13 shorter events, 0.1 us)
Async XLA Ops:
  8.0 144.7 %all-gather.3.cloned.1.call-start = ((), (), s32[]{:S(2)}) async-start(), calls=%async_computation.2 | async-start | bytes 1081344 | tf_op jit(solution)/shard_map/all_gather | solution.py:46
  9.4 462.8 %all-reduce.2.cloned.1.call-start = ((), (), s32[]{:S(2)}) async-start(), calls=%async_computation.4 | async-start | bytes 393216 | tf_op jit(solution)/shard_map/psum | solution.py:93
  95.8 1.9 copy-start.6
  95.8 56.8 %copy-start.2 = (bf16[128,64]{0,1:T(8,128)(2,1)S(1)}, bf16[128,64]{0,1:T(8,128)(2,1)}, u32[]{:S(2)}) copy-start(bf16[128,64]{0,1:T(8,128)(2,1)} %param.7) | copy-start | bytes 49156
  152.7 3.0 copy-start
  155.6 6.3 %copy-start.5 = (bf16[8,1536]{1,0:T(8,128)(2,1)S(1)}, bf16[8,1536]{1,0:T(8,128)(2,1)}, u32[]{:S(2)}) copy-start(bf16[8,1536]{1,0:T(8,128)(2,1)} %param.13) | copy-start | bytes 73732
  155.6 25.9 %copy-start.1 = (bf16[64,1536]{1,0:T(8,128)(2,1)S(1)}, bf16[64,1536]{1,0:T(8,128)(2,1)}, u32[]{:S(2)}) copy-start(bf16[64,1536]{1,0:T(8,128)(2,1)} %param.12) | copy-start | bytes 589828
  156.0 23.4 %collective-permute-start.1 = (bf16[16,64]{0,1:T(8,128)(2,1)S(1)}, bf16[16,64]{0,1:T(8,128)(2,1)S(1)}, u32[]{:S(2)}, u32[]{:S(2)}) collective-permute-start(bf16[16,64]{0,1:T(8,128)(2,1)S(1)} %get-tuple-element.79), channel_id=1, source_target_pairs={{16,0},{32,16},{48,32},{64,48},{80,64},{96,80},{112,96},{128,112},... | collective-permute-start | bytes 6152 | tf_op jit(solution)/shard_map/ppermute | solution.py:17
  157.3 22.1 %collective-permute-start = (bf16[16,64]{0,1:T(8,128)(2,1)S(1)}, bf16[16,64]{0,1:T(8,128)(2,1)S(1)}, u32[]{:S(2)}, u32[]{:S(2)}) collective-permute-start(bf16[16,64]{0,1:T(8,128)(2,1)S(1)} %get-tuple-element.78), channel_id=1, source_target_pairs={{0,16},{16,32},{32,48},{48,64},{64,80},{80,96},{96,112},{112,128},... | collective-permute-start | bytes 6152 | tf_op jit(solution)/shard_map/ppermute | solution.py:14
  181.0 293.0 %all-gather.5.cloned.1.call-start = ((), (), s32[]{:S(2)}) async-start(), calls=%async_computation.3 | async-start | bytes 3342336 | tf_op jit(solution)/shard_map/all_gather | solution.py:69
  182.1 11.3 %collective-permute-start.3 = (bf16[16,64]{0,1:T(8,128)(2,1)S(1)}, bf16[16,64]{0,1:T(8,128)(2,1)S(1)}, u32[]{:S(2)}, u32[]{:S(2)}) collective-permute-start(bf16[16,64]{0,1:T(8,128)(2,1)S(1)} %get-tuple-element.45), channel_id=1, source_target_pairs={{0,16},{16,32},{32,48},{48,64},{64,80},{80,96},{96,112},{112,128},... | collective-permute-start | bytes 6152 | tf_op jit(solution)/shard_map/ppermute | solution.py:14
  185.3 8.1 %collective-permute-start.2 = (bf16[16,64]{0,1:T(8,128)(2,1)S(1)}, bf16[16,64]{0,1:T(8,128)(2,1)S(1)}, u32[]{:S(2)}, u32[]{:S(2)}) collective-permute-start(bf16[16,64]{0,1:T(8,128)(2,1)S(1)} %get-tuple-element.44), channel_id=1, source_target_pairs={{16,0},{32,16},{48,32},{64,48},{80,64},{96,80},{112,96},{128,112},... | collective-permute-start | bytes 6152 | tf_op jit(solution)/shard_map/ppermute | solution.py:17
  187.4 10.8 %all-to-all-start = ((bf16[16,2,256]{2,1,0:T(2,128)(2,1)}), bf16[16,2,256]{2,1,0:T(2,128)(2,1)S(1)}, u32[]{:S(2)}, u32[]{:S(2)}) async-start(bf16[16,2,256]{2,1,0:T(2,128)(2,1)} %reshape.56), calls=%async_computation | async-start | bytes 32768 | tf_op jit(solution)/shard_map/all_to_all | solution.py:68
  199.4 277.5 %all-to-all-start.1 = ((bf16[32,128,128]{2,1,0:T(8,128)(2,1)}), bf16[32,128,128]{2,1,0:T(8,128)(2,1)S(1)}, u32[]{:S(2)}, u32[]{:S(2)}) async-start(bf16[32,128,128]{2,1,0:T(8,128)(2,1)} %stack.172), calls=%async_computation.1 | async-start | bytes 2097152 | tf_op jit(solution)/shard_map/all_to_all | solution.py:128
  401.0 76.0 %copy-start.4 = (bf16[128,64]{0,1:T(8,128)(2,1)S(1)}, bf16[128,64]{0,1:T(8,128)(2,1)}, u32[]{:S(2)}) copy-start(bf16[128,64]{0,1:T(8,128)(2,1)} %param.8) | copy-start | bytes 49156
  477.8 1.6 copy-start.3
Sparse Core Ops, SparseCore 0:
  12.3 140.2 all-gather.2
  181.1 291.1 all-reduce.1
Sparse Core Ops, SparseCore 1:
  183.6 39.5 all-gather.4
